TPU v7x, 512 devices: a whole 4x8x8 slice. The times are simulated.
512 devices in a mesh: rep: 8 (over y_lo, core), shard: 64 (over y_hi, z, x).
Axes of the slice: x: 4, y: 8 (y_hi: 2, y_lo: 4; y = y_hi * 4 + y_lo), z: 8, core: 2. Of those that a mesh axis runs over, the one named last changes fastest.
Arguments:
- grad_parts: bfloat16 [8, 64, 576, 1152], P('rep', 'shard'), may hold values from -64 to 64
- master: float32 [576, 1152], P('shard'), may hold values from -0.06 to 0.06
- moment_one: float32 [576, 1152], P('shard'), may hold values from -0.12 to 0.12
- moment_two: float32 [576, 1152], P('shard'), may hold values from 0.0001 to 0.01
- step_count: int32 [1], replicated, may hold values from 1 to 20
Outputs:
- new_master: float32 [576, 1152], P('shard')
- new_moment_one: float32 [576, 1152], P('shard')
- new_moment_two: float32 [576, 1152], P('shard')
- adam_direction: float32 [576, 1152], P('shard')
- params: bfloat16 [576, 1152], replicated
All inputs are finite; a program needn't handle non-finite values.
Results may differ from a plain program's by a relative error of at most 0.024.
Values may be sent and summed in bfloat16 or wider, within the bound.
A program may use at most 64 MiB of HBM per device.

v0:
```python
import jax
import jax.numpy as jnp
from jax import lax
from jax.sharding import PartitionSpec as P

BETA_ONE = 0.9
BETA_TWO = 0.95
LEARN_RATE = 0.001
EPSILON = 1e-08


def adam_step(gradient, master, moment_one, moment_two, step_count):
    new_moment_one = BETA_ONE * moment_one + (1.0 - BETA_ONE) * gradient
    new_moment_two = BETA_TWO * moment_two + (1.0 - BETA_TWO) * gradient * gradient
    steps_float = step_count[0].astype(jnp.float32)
    first_fix = 1.0 - jnp.power(jnp.float32(BETA_ONE), steps_float)
    second_fix = 1.0 - jnp.power(jnp.float32(BETA_TWO), steps_float)
    direction = new_moment_one / first_fix / (jnp.sqrt(new_moment_two / second_fix) + EPSILON)
    new_master = master - LEARN_RATE * direction
    return (new_master, new_moment_one, new_moment_two, direction)


def local(grad_parts, master, moment_one, moment_two, step_count):
    partial_value = grad_parts.reshape(grad_parts.shape[2], grad_parts.shape[3]).astype(jnp.float32)
    devices_total = lax.axis_size("rep") * lax.axis_size("shard")
    row_block = lax.psum_scatter(partial_value, "shard", scatter_dimension=0, tiled=True)
    summed = lax.psum(row_block, "rep")
    results = adam_step(summed / devices_total, master, moment_one, moment_two, step_count)
    new_master, new_moment_one, new_moment_two, direction = results
    params = lax.all_gather(new_master.astype(jnp.bfloat16), "shard", axis=0, tiled=True)
    return (new_master, new_moment_one, new_moment_two, direction, params)


def solution(mesh):
    placed = (
        P("rep", "shard", None, None),
        P("shard", None),
        P("shard", None),
        P("shard", None),
        P(),
    )
    return jax.shard_map(
        local,
        mesh=mesh,
        in_specs=placed,
        out_specs=(P("shard", None), P("shard", None), P("shard", None), P("shard", None), P()),
        check_vma=False,
    )
```

profile of v0, /device:TPU:8, one launch (start us, length us, event | category | flops | bytes accessed | tf_op | source)
XLA Modules:
  0.0 1022.8 jit_solution(6413098635314897203)
XLA Ops:
  7.2 0.0 copy-start
  7.2 0.0 copy-start.2
  7.2 0.0 copy-start.1
  7.2 0.0 all-reduce.3.cloned.1.call-start
  7.2 3.1 bitcast_convert_fusion
  10.3 0.0 all-reduce.3.cloned.1.call-update
  10.3 0.0 all-gather.3.cloned.1.call-start
  11.1 1.3 dynamic-slice
  13.0 837.0 %all-reduce.3.cloned.1.call-done = f32[576,1152]{1,0:T(8,128)} async-done(((f32[576,1152]{1,0:T(8,128)}), f32[576,1152]{1,0:T(8,128)}) %all-reduce.3.cloned.1.call-update) | async-done | bytes 2654224
  850.1 0.9 constant_dynamic-slice_fusion
  851.0 23.2 %psum.7 = f32[9,1152]{1,0:T(8,128)S(1)} all-reduce(f32[9,1152]{1,0:T(8,128)S(1)} %constant_dynamic-slice_fusion), channel_id=1, replica_groups=mesh['rep'=8,'shard'=64] {'rep'}, use_global_device_ids=true, to_apply=%region_1.0 | all-reduce | flops 10368 | bytes 82944 | tf_op jit(solution)/shard_map/psum | solution.py:27
  874.2 0.0 copy-done
  874.2 0.0 copy-done.2
  874.2 0.0 copy-done.1
  874.2 0.7 convert_bitcast_fusion
  874.9 0.0 all-gather.3.cloned.1.call-update
  875.0 137.3 %all-gather.3.cloned.1.call-done = bf16[64,9,1152]{2,1,0:T(8,128)(2,1)} async-done(((bf16[1,9,1152]{2,1,0:T(8,128)(2,1)}), bf16[64,9,1152]{2,1,0:T(8,128)(2,1)}) %all-gather.3.cloned.1.call-update) | async-done | bytes 1327120 | tf_op jit(solution)/shard_map/all_gather | solution.py:30
  1012.2 3.7 reshape.24
Async XLA Ops:
  7.2 867.0 %copy-start = (f32[9,1152]{1,0:T(8,128)S(1)}, f32[9,1152]{1,0:T(8,128)}, u32[]{:S(2)}) copy-start(f32[9,1152]{1,0:T(8,128)} %param.6) | copy-start | bytes 124420
  7.2 867.0 %copy-start.2 = (f32[9,1152]{1,0:T(8,128)S(1)}, f32[9,1152]{1,0:T(8,128)}, u32[]{:S(2)}) copy-start(f32[9,1152]{1,0:T(8,128)} %param.7) | copy-start | bytes 124420
  7.2 867.0 %copy-start.1 = (f32[9,1152]{1,0:T(8,128)S(1)}, f32[9,1152]{1,0:T(8,128)}, u32[]{:S(2)}) copy-start(f32[9,1152]{1,0:T(8,128)} %param.8) | copy-start | bytes 124420
  7.2 842.9 %all-reduce.3.cloned.1.call-start = ((), (), s32[]{:S(2)}) async-start(), calls=%async_computation.1 | async-start | bytes 5308416
  10.3 1001.9 %all-gather.3.cloned.1.call-start = ((), (), s32[]{:S(2)}) async-start(), calls=%async_computation | async-start | bytes 2396160 | tf_op jit(solution)/shard_map/all_gather | solution.py:30
Sparse Core Ops, SparseCore 0:
  11.0 839.0 all-reduce.2
  875.1 137.1 all-gather.2
where the time goes:
time: 1020 us
  waiting for transfers between devices  974 us (95%)
  blocking collectives  23.2 us (2%)
  between operations  15.5 us (2%)
    unnamed x3, waiting for transfers between devices  837 us
    all_gather x1, waiting for transfers between devices, local(): lax.all_gather(new_master.astype(jnp.bfloat16), 'shard', axis=0, tiled=True)  137 us
    psum x1, blocking collectives, local(): summed = lax.psum(row_block, 'rep')  23.2 us
  transfers between devices with their start and end apart: 2, of which 2 were waited for; matrix products, arithmetic and copies ran while one was open for 0% of the time, Pallas kernels for 0%

commit v1 on v0

--- a/solution.py
+++ b/solution.py
@@ -27,7 +27,11 @@
     summed = lax.psum(row_block, "rep")
     results = adam_step(summed / devices_total, master, moment_one, moment_two, step_count)
     new_master, new_moment_one, new_moment_two, direction = results
-    params = lax.all_gather(new_master.astype(jnp.bfloat16), "shard", axis=0, tiled=True)
+    payload = new_master.astype(jnp.bfloat16)
+    local_now = lax.axis_size("shard")
+    params = jnp.concatenate(
+        lax.all_to_all(jnp.stack([payload] * local_now), "shard", 0, 0), axis=0
+    )
     return (new_master, new_moment_one, new_moment_two, direction, params)
 
 

time: 1020 us -> 956 us (0.937)
  the two profiles are of different devices: /device:TPU:8 before, /device:TPU:30 now
where the time goes in v1:
time: 956 us; the launch traced here: 955 us
  waiting for transfers between devices  829 us (87%)
  blocking collectives  104 us (11%)
  between operations  15.5 us (2%)
    unnamed x2, waiting for transfers between devices  829 us
    all_to_all x1, blocking collectives, local(): lax.all_to_all(jnp.stack([payload] * local_now), 'shard', 0, 0)  79.5 us
    psum x1, blocking collectives, local(): summed = lax.psum(row_block, 'rep')  24.1 us
  transfers between devices with their start and end apart: 1, of which 1 were waited for; matrix products, arithmetic and copies ran while one was open for 0% of the time, Pallas kernels for 0%

profile of v1, /device:TPU:30, one launch (start us, length us, event | category | flops | bytes accessed | tf_op | source)
XLA Modules:
  0.0 955.5 jit_solution(9978984103658960192)
XLA Ops:
  7.2 0.0 all-reduce.3.cloned.1.call-start
  7.2 3.0 bitcast_convert_fusion
  10.2 0.0 copy-start
  10.2 0.0 copy-start.1
  10.2 0.0 copy-start.2
  10.2 0.0 all-reduce.3.cloned.1.call-update
  11.0 1.3 dynamic-slice
  13.0 828.8 %all-reduce.3.cloned.1.call-done = f32[576,1152]{1,0:T(8,128)} async-done(((f32[576,1152]{1,0:T(8,128)}), f32[576,1152]{1,0:T(8,128)}) %all-reduce.3.cloned.1.call-update) | async-done | bytes 2654224
  841.7 0.9 constant_dynamic-slice_fusion
  842.6 24.1 %psum.7 = f32[9,1152]{1,0:T(8,128)S(1)} all-reduce(f32[9,1152]{1,0:T(8,128)S(1)} %constant_dynamic-slice_fusion), channel_id=1, replica_groups=mesh['rep'=8,'shard'=64] {'rep'}, use_global_device_ids=true, to_apply=%region_1.0 | all-reduce | flops 10368 | bytes 82944 | tf_op jit(solution)/shard_map/psum | solution.py:27
  866.8 0.0 copy-done
  866.8 0.0 copy-done.1
  866.8 0.0 copy-done.2
  866.8 0.7 fusion
  867.6 0.2 stack.2
  867.7 79.5 %all_to_all.5 = bf16[64,9,1152]{2,1,0:T(8,128)(2,1)S(1)} all-to-all(bf16[64,9,1152]{2,1,0:T(8,128)(2,1)S(1)} %stack.2), channel_id=1, replica_groups=mesh['rep'=8,'shard'=64] {'shard'}, dimensions={0} | all-to-all | bytes 2654208 | tf_op jit(solution)/shard_map/all_to_all | solution.py:33
  947.2 1.4 reshape.27
Async XLA Ops:
  7.2 834.6 %all-reduce.3.cloned.1.call-start = ((), (), s32[]{:S(2)}) async-start(), calls=%async_computation.1 | async-start | bytes 5308416
  10.2 856.6 %copy-start = (f32[9,1152]{1,0:T(8,128)S(1)}, f32[9,1152]{1,0:T(8,128)}, u32[]{:S(2)}) copy-start(f32[9,1152]{1,0:T(8,128)} %param.6) | copy-start | bytes 124420
  10.2 856.6 %copy-start.1 = (f32[9,1152]{1,0:T(8,128)S(1)}, f32[9,1152]{1,0:T(8,128)}, u32[]{:S(2)}) copy-start(f32[9,1152]{1,0:T(8,128)} %param.8) | copy-start | bytes 124420
  10.2 856.6 %copy-start.2 = (f32[9,1152]{1,0:T(8,128)S(1)}, f32[9,1152]{1,0:T(8,128)}, u32[]{:S(2)}) copy-start(f32[9,1152]{1,0:T(8,128)} %param.7) | copy-start | bytes 124420
Sparse Core Ops, SparseCore 0:
  10.9 830.7 all-reduce.2
